TPU v7x, 256 devices: a whole 4x4x8 slice. The times are simulated.
256 devices in a mesh: row: 64 (over z, y, core), col: 4 (over x).
Axes of the slice: x: 4, y: 4, z: 8, core: 2. Of those that a mesh axis runs over, the one named last changes fastest.
Arguments:
- row_embed: float32 [65536, 512], P(('row', 'col')), may hold values from -1.5 to 1.5
- row_accum: float32 [65536, 512], P(('row', 'col')), may hold values from 0.001 to 0.01
- col_embed: float32 [4, 4096, 512], P('col', 'row'), may hold values from -1.5 to 1.5
- col_accum: float32 [4, 4096, 512], P('col', 'row'), may hold values from 0.001 to 0.01
- col_freq: int32 [4, 4096], P('col'), may hold values from 1000 to 29999
- row_freq: int32 [65536], P('row'), may hold values from 1000 to 29999
- block_cols: int32 [64, 4, 2], P('row', 'col'), may hold values from 0 to 3, all different within a row
- counts: int32 [64, 4, 2, 1024, 1024], P('row', 'col'), may hold values from 0 to 1024
- excluded: int32 [512], replicated, may hold values from 0 to 65535
- log_total: float32 [], replicated, may hold values from 15 to 19
Outputs:
- row_embed_new: float32 [65536, 512], P(('row', 'col'))
- row_accum_new: float32 [65536, 512], P(('row', 'col'))
- col_embed_new: float32 [4, 4096, 512], P('col', 'row')
- col_accum_new: float32 [4, 4096, 512], P('col', 'row')
Inputs may be any that keep to these rules, and one draw needn't show every extreme that they name: `block_cols`: the 2 column blocks of one row block and group are different.
All inputs are finite; a program needn't handle non-finite values.
Results may differ from a plain program's by a relative error of at most 0.0071.
The roundings to bfloat16 on the way count: a program that leaves them out, or rounds other values in their place, can miss the bound.
Values may be sent and summed in bfloat16 or wider, within the bound.
A program may use at most 128 MiB of HBM per device.

v0:
```python
import jax
import jax.numpy as jnp
from jax import lax
from jax.sharding import PartitionSpec as P

BLOCK = 1024
learn_rate = 0.2
decay_rate = 0.5


def cell_grads(count_block, predicted, row_logs, col_logs, log_total):
    nonzero = count_block > 0
    safe_count = jnp.where(nonzero, count_block.astype(jnp.float32), jnp.float32(1.0))
    baseline = log_total - row_logs[:, None] - col_logs[None, :]
    weight = 0.1 + 0.25 * jnp.sqrt(safe_count)
    fitted = weight * (predicted - baseline - jnp.log(safe_count))
    hinge_grad = jax.nn.sigmoid(predicted - baseline)
    return (jnp.where(nonzero, fitted, hinge_grad) / BLOCK).astype(jnp.bfloat16)


def body(
    row_embed,
    row_accum,
    col_embed,
    col_accum,
    col_freq,
    row_freq,
    block_cols,
    counts,
    excluded,
    log_total,
):
    block = counts.shape[3]
    slots = counts.shape[2]
    width = row_embed.shape[1]
    own_rows = row_embed.shape[0]
    own_cols = col_embed.shape[1]
    chosen = block_cols[0, 0]
    block_rows = lax.all_gather(row_embed.astype(jnp.bfloat16), "col", axis=0, tiled=True)
    piece = lax.all_gather(col_embed.astype(jnp.bfloat16), "row", axis=1, tiled=True)
    span = piece.shape[1]
    positions = jnp.arange(span, dtype=jnp.int32)
    owner_block = positions // block
    offset = positions - owner_block * block
    target = jnp.full((span,), slots * block, jnp.int32)
    for collect_slot_id in range(slots):
        target = jnp.where(
            owner_block == chosen[collect_slot_id], collect_slot_id * block + offset, target
        )
    fetched = jnp.zeros((slots * block, width), jnp.bfloat16).at[target].set(piece[0], mode="drop")
    row_logs = jnp.log(row_freq.astype(jnp.float32))
    col_logs = jnp.log(col_freq[0].astype(jnp.float32))
    row_grad = jnp.zeros((block, width), jnp.float32)
    col_parts = []
    for slot_id in range(slots):
        col_block = fetched[slot_id * block : (slot_id + 1) * block]
        block_col_logs = lax.dynamic_slice_in_dim(col_logs, chosen[slot_id] * block, block)
        predicted = lax.dot_general(
            block_rows, col_block, (((1,), (1,)), ((), ())), preferred_element_type=jnp.float32
        )
        cell = cell_grads(counts[0, 0, slot_id], predicted, row_logs, block_col_logs, log_total)
        row_grad = row_grad + jnp.dot(cell, col_block, preferred_element_type=jnp.float32)
        col_parts.append(
            lax.dot_general(
                cell, block_rows, (((0,), (0,)), ((), ())), preferred_element_type=jnp.float32
            )
        )
    positions = jnp.arange(own_cols * lax.axis_size("row"), dtype=jnp.int32)
    owner_block = positions // block
    offset = positions - owner_block * block
    summed = jnp.zeros((own_cols * lax.axis_size("row"), width), jnp.float32)
    for slot_id in range(slots):
        picked = jnp.take(col_parts[slot_id], offset, axis=0)
        summed = summed + jnp.where(
            (owner_block == chosen[slot_id])[:, None], picked, jnp.float32(0.0)
        )
    col_grad = lax.psum_scatter(summed, "row", scatter_dimension=0, tiled=True)
    own_grad = lax.psum_scatter(row_grad, "col", scatter_dimension=0, tiled=True)
    col_index = lax.axis_index("col")
    row_index = lax.axis_index("row")
    own_freq = lax.dynamic_slice_in_dim(row_freq, col_index * own_rows, own_rows).astype(
        jnp.float32
    )
    row_ids = row_index * block + col_index * own_rows + jnp.arange(own_rows, dtype=jnp.int32)
    decayed = jnp.all(row_ids[:, None] != excluded[None, :], axis=1)
    freq_root = jnp.sqrt(own_freq)
    decay_coef = jnp.where(decayed, decay_rate * freq_root / (freq_root + 30.0), jnp.float32(0.0))
    full_grad = own_grad + decay_coef[:, None] * row_embed
    row_accum_new = row_accum + full_grad * full_grad
    row_embed_new = row_embed - learn_rate * full_grad / jnp.sqrt(row_accum_new)
    col_step = col_grad[None]
    col_accum_new = col_accum + col_step * col_step
    col_embed_new = col_embed - learn_rate * col_step / jnp.sqrt(col_accum_new)
    return (row_embed_new, row_accum_new, col_embed_new, col_accum_new)


def solution(mesh):
    in_specs = (
        P(("row", "col"), None),
        P(("row", "col"), None),
        P("col", "row", None),
        P("col", "row", None),
        P("col", None),
        P("row"),
        P("row", "col", None),
        P("row", "col", None, None, None),
        P(),
        P(),
    )
    out_specs = (
        P(("row", "col"), None),
        P(("row", "col"), None),
        P("col", "row", None),
        P("col", "row", None),
    )
    return jax.shard_map(body, mesh=mesh, in_specs=in_specs, out_specs=out_specs, check_vma=False)
```

profile of v0, /device:TPU:2, one launch (start us, length us, event | category | flops | bytes accessed | tf_op | source)
XLA Modules:
  0.0 349.1 jit_solution(11396950544478308842)
XLA Ops:
  7.2 1.5 convert_element_type.36
  8.8 1.8 convert_element_type.37
  10.7 1.3 fusion.20
  13.3 8.3 %fusion.19 = (s32[1,1,1,1024,1024]{4,3,2,1,0:T(8,128)}, s32[1,1,1,1024,1024]{4,3,2,1,0:T(8,128)}) fusion(s32[1,1,2,1024,1024]{4,3,2,1,0:T(8,128)} %param.19), kind=kLoop, calls=%fused_computation.56 | loop fusion | bytes 16777216 | tf_op jit(solution)/shard_map/slice | solution.py:61
  21.7 5.4 %copy.20 = s32[1,1,1,1024,1024]{3,4,2,1,0:T(8,128)} copy(s32[1,1,1,1024,1024]{4,3,2,1,0:T(8,128)} %get-tuple-element.10) | data formatting | bytes 8388608
  27.7 5.4 %copy.21 = s32[1,1,1,1024,1024]{3,4,2,1,0:T(8,128)} copy(s32[1,1,1,1024,1024]{4,3,2,1,0:T(8,128)} %get-tuple-element.9) | data formatting | bytes 8388608
  33.2 1.4 compare_select_fusion
  34.5 58.8 %all-gather.3.cloned.1.call-done = bf16[1,4096,512]{2,1,0:T(8,128)(2,1)} async-done(((bf16[1,64,512]{2,1,0:T(8,128)(2,1)}), bf16[1,4096,512]{2,1,0:T(8,128)(2,1)}) %all-gather.3.cloned.1.call-update) | async-done | bytes 4194320 | tf_op jit(solution)/shard_map/all_gather | solution.py:40
  93.4 19.2 %scatter_custom_fusion = bf16[2048,512]{1,0:T(8,128)(2,1)S(1)} fusion(s32[4096]{0:T(1024)S(1)} %bitcast.43, bf16[1,4096,512]{2,1,0:T(8,128)(2,1)} %all-gather.3.cloned.1.call-done, bf16[]{:T(256)} %constant.64.clone.1), kind=kCustom, calls=%fused_computation.9 | custom fusion | bytes 6291458 | tf_op jit(solution)/shard_map/scatter | solution.py:50
  112.6 6.0 %all-gather.5.cloned.1.call-done = bf16[1024,512]{1,0:T(8,128)(2,1)} async-done(((bf16[256,512]{1,0:T(8,128)(2,1)}), bf16[1024,512]{1,0:T(8,128)(2,1)}) %all-gather.5.cloned.1.call-update) | async-done | bytes 1048592 | tf_op jit(solution)/shard_map/all_gather | solution.py:39
  118.6 7.2 %multiply_convert_fusion.1 = bf16[1024,1024]{0,1:T(8,128)(2,1)S(1)} fusion(s32[1,1,1,1024,1024]{3,4,2,1,0:T(8,128)} %copy.20, bf16[1024,512]{1,0:T(8,128)(2,1)} %all-gather.5.cloned.1.call-done, f32[1024]{0:T(1024)S(1)} %bitcast.45, f32[1024]{0:T(1024)S(1)} %log_subtract_fusion, bf16[2048,512]{1,0:T(8,128)(2,1)S(1)} %scatter_custom_fusion), kind=kOutput, calls=%fused_computation.13 | convolution fusion | flops 1089470464 | bytes 8396800 | tf_op jit(solution)/shard_map/dot_general | solution.py:58
  125.9 1.3 fusion.6
  127.2 1.6 copy-done
  128.8 0.3 copy-done.8
  129.1 4.1 %multiply_convert_fusion = bf16[1024,1024]{0,1:T(8,128)(2,1)S(1)} fusion(s32[1,1,1,1024,1024]{3,4,2,1,0:T(8,128)S(1)} %copy-done, bf16[1024,512]{1,0:T(8,128)(2,1)S(1)} %copy-done.8, f32[1024]{0:T(1024)S(1)} %bitcast.44, f32[1024]{0:T(1024)S(1)} %log_subtract_fusion, bf16[2048,512]{1,0:T(8,128)(2,1)S(1)} %scatter_custom_fusion), kind=kOutput, calls=%fused_computation.12 | convolution fusion | flops 1089470464 | bytes 8396800 | tf_op jit(solution)/shard_map/dot_general | solution.py:58
  133.3 1.3 copy-done.9
  134.6 2.6 convolution_add_fusion
  137.2 0.2 reduce-scatter.5.cloned.1.call-start
  137.5 1.3 fusion.12
  138.8 2.8 fusion.22
  141.6 16.8 %gather_fusion.1 = f32[4096,512]{1,0:T(8,128)} fusion(f32[1024,512]{1,0:T(8,128)S(1)} %fusion.22, s32[4096]{0:T(1024)S(1)} %fusion.17), kind=kCustom, calls=%fused_computation.1.clone | custom fusion | bytes 16793600 | tf_op jit(solution)/shard_map/jit(_take)/gather | solution.py:73
  158.4 2.8 fusion.21
  161.3 16.8 %gather_fusion = f32[4096,512]{1,0:T(8,128)} fusion(f32[1024,512]{1,0:T(8,128)S(1)} %fusion.21, s32[4096]{0:T(1024)S(1)} %fusion.17), kind=kCustom, calls=%fused_computation.clone | custom fusion | bytes 16793600 | tf_op jit(solution)/shard_map/jit(_take)/gather | solution.py:73
  178.1 9.9 %fusion = f32[4096,512]{1,0:T(8,128)} fusion(f32[4096,512]{1,0:T(8,128)} %gather_fusion.1, f32[4096,512]{1,0:T(8,128)} %gather_fusion, pred[4096]{0:T(1024)(128)(4,1)S(1)} %compare_and_fusion, pred[4096]{0:T(1024)(128)(4,1)S(1)} %get-tuple-element.15, pred[4096]{0:T(1024)(128)(4,1)S(1)} %get-tuple-element.16), kind=kLoop, calls=%fused_computation.4 | loop fusion | flops 10485760 | bytes 25178112 | tf_op jit(solution)/shard_map/add | solution.py:74
  188.1 0.6 copy-done.7
  188.7 0.2 compare_reduce_fusion
  188.9 0.1 fusion.18
  188.9 0.1 copy-done.1
  189.1 0.2 copy-done.2
  189.2 2.2 multiply_subtract_fusion
  191.4 149.5 %reduce-scatter.5.cloned.1.call-done = f32[64,512]{1,0:T(8,128)} async-done(((f32[4096,512]{1,0:T(8,128)}), f32[64,512]{1,0:T(8,128)}) %reduce-scatter.5.cloned.1.call-update) | async-done | bytes 131088 | tf_op jit(solution)/shard_map/reduce_scatter | solution.py:77
  340.9 1.6 fusion.9
  (30 shorter events, 0.3 us)
Async XLA Ops:
  7.2 86.2 %all-gather.3.cloned.1.call-start = ((), (), s32[]{:S(2)}) async-start(), calls=%async_computation.2 | async-start | bytes 4259840 | tf_op jit(solution)/shard_map/all_gather | solution.py:40
  8.8 109.9 %all-gather.5.cloned.1.call-start = ((), (), s32[]{:S(2)}) async-start(), calls=%async_computation.3 | async-start | bytes 1310720 | tf_op jit(solution)/shard_map/all_gather | solution.py:39
  10.6 178.3 %reduce-scatter.3.cloned.1.call-start = ((), (), s32[]{:S(2)}) async-start(), calls=%async_computation.4 | async-start | bytes 2621440 | tf_op jit(solution)/shard_map/reduce_scatter | solution.py:78
  27.7 5.4 %copy-start.5 = (s32[1,4096]{1,0:T(1,128)S(1)}, s32[1,4096]{1,0:T(1,128)}, u32[]{:S(2)}) copy-start(s32[1,4096]{1,0:T(1,128)} %param.16) | copy-start | bytes 49156
  27.7 5.4 %copy-start.6 = (s32[1024]{0:T(1024)S(1)}, s32[1024]{0:T(1024)}, u32[]{:S(2)}) copy-start(s32[1024]{0:T(1024)} %param.17) | copy-start | bytes 12292
  125.9 1.3 copy-start.10
  125.9 2.9 copy-start
  125.9 3.2 copy-start.8
  133.3 1.3 copy-start.9
  137.2 203.7 %reduce-scatter.5.cloned.1.call-start = ((), (), s32[]{:S(2)}) async-start(), calls=%async_computation.5 | async-start | bytes 8519680 | tf_op jit(solution)/shard_map/reduce_scatter | solution.py:77
  188.0 0.7 copy-start.7
  188.0 1.1 copy-start.1
  188.0 1.2 copy-start.2
  188.0 152.9 %copy-start.3 = (f32[1,64,512]{2,1,0:T(8,128)S(1)}, f32[1,64,512]{2,1,0:T(8,128)}, u32[]{:S(2)}) copy-start(f32[1,64,512]{2,1,0:T(8,128)} %param.14) | copy-start | bytes 393220
  188.0 152.9 %copy-start.4 = (f32[1,64,512]{2,1,0:T(8,128)S(1)}, f32[1,64,512]{2,1,0:T(8,128)}, u32[]{:S(2)}) copy-start(f32[1,64,512]{2,1,0:T(8,128)} %param.15) | copy-start | bytes 393220
Sparse Core Ops, SparseCore 0:
  11.3 81.9 all-gather.2
  95.7 22.8 all-gather.4
  137.3 32.1 reduce-scatter.2
  188.2 152.6 reduce-scatter.4
where the time goes:
time: 350 us; the launch traced here: 349 us
  waiting for transfers between devices  214 us (61%)
  local copies, waits for them, and re-layouts  77.4 us (22%)
  matrix products  20.9 us (6%)
  other arithmetic  20.1 us (6%)
  between operations  15.9 us (5%)
    reduce_scatter x1, waiting for transfers between devices, body(): col_grad = lax.psum_scatter(summed, 'row', scatter_dimension=0, tiled=True)  149 us
    all_gather x1, waiting for transfers between devices, body(): lax.all_gather(col_embed.astype(jnp.bfloat16), 'row', axis=1, tiled=True)  58.8 us
    gather x2, local copies, waits for them, and re-layouts, body(): picked = jnp.take(col_parts[slot_id], offset, axis=0)  33.6 us
    scatter x1, local copies, waits for them, and re-layouts, body(): jnp.zeros((slots * block, width), jnp.bfloat16).at[target]  19.2 us
    unnamed x24, local copies, waits for them, and re-layouts  14.9 us
    dot_general x2, matrix products, body(): lax.dot_general(block_rows, col_block, (((1,), (1,)), ((), ())), preferre...  11.4 us
    add x1, other arithmetic, body(): summed + jnp.where((owner_block == chosen[slot_id])[:, None], picked, jnp...  9.91 us
    slice x1, local copies, waits for them, and re-layouts, body(): counts[0, 0, slot_id]  8.35 us
  transfers between devices with their start and end apart: 4, of which 3 were waited for; matrix products, arithmetic and copies ran while one was open for 27% of the time, Pallas kernels for 0%

commit v1 on v0

--- a/solution.py
+++ b/solution.py
@@ -37,7 +37,12 @@
     own_cols = col_embed.shape[1]
     chosen = block_cols[0, 0]
     block_rows = lax.all_gather(row_embed.astype(jnp.bfloat16), "col", axis=0, tiled=True)
-    piece = lax.all_gather(col_embed.astype(jnp.bfloat16), "row", axis=1, tiled=True)
+    piece = jnp.concatenate(
+        lax.all_to_all(
+            jnp.stack([col_embed.astype(jnp.bfloat16)] * lax.axis_size("row")), "row", 0, 0
+        ),
+        axis=1,
+    )
     span = piece.shape[1]
     positions = jnp.arange(span, dtype=jnp.int32)
     owner_block = positions // block

time: 350 us -> 365 us (1.043)
  starting transfers between devices: 0.34 us -> 12.6 us
    all_to_all x0 -> x1, waiting for transfers between devices: none -> 72.3 us  [body(): lax.all_to_all(jnp.stack([col_embed.astype(jnp.bfloat16)] * lax.axis_size...]
    all_gather x1 -> x0, waiting for transfers between devices: 58.8 us -> none  [body(): lax.all_gather(col_embed.astype(jnp.bfloat16), 'row', axis=1, tiled=True)]
    all_to_all x0 -> x1, starting transfers between devices: none -> 12.5 us  [body(): lax.all_to_all(jnp.stack([col_embed.astype(jnp.bfloat16)] * lax.axis_size...]
    all_gather x1, waiting for transfers between devices: 6.05 us -> 0.02 us  [body(): lax.all_gather(row_embed.astype(jnp.bfloat16), 'col', axis=0, tiled=True)]
    reduce_scatter x1, waiting for transfers between devices: 149 us -> 144 us  [body(): col_grad = lax.psum_scatter(summed, 'row', scatter_dimension=0, tiled=True)]
    unnamed x24 -> x26, local copies, waits for them, and re-layouts: 14.9 us -> 14.8 us
  transfers between devices with their start and end apart: 4 -> 4, of which waited for: 3 -> 2; matrix products, arithmetic and copies ran while one was open for 27% -> 26% of each run, Pallas kernels for 0% -> 0%
where the time goes in v1:
time: 365 us
  waiting for transfers between devices  217 us (59%)
  local copies, waits for them, and re-layouts  79.2 us (22%)
  matrix products  21.8 us (6%)
  other arithmetic  18.4 us (5%)
  between operations  15.9 us (4%)
  starting transfers between devices  12.6 us (3%)
    reduce_scatter x1, waiting for transfers between devices, body(): col_grad = lax.psum_scatter(summed, 'row', scatter_dimension=0, tiled=True)  144 us
    all_to_all x1, waiting for transfers between devices, body(): lax.all_to_all(jnp.stack([col_embed.astype(jnp.bfloat16)] * lax.axis_size...  72.3 us
    gather x2, local copies, waits for them, and re-layouts, body(): picked = jnp.take(col_parts[slot_id], offset, axis=0)  33.6 us
    scatter x1, local copies, waits for them, and re-layouts, body(): jnp.zeros((slots * block, width), jnp.bfloat16).at[target]  19.4 us
    unnamed x26, local copies, waits for them, and re-layouts  14.8 us
    all_to_all x1, starting transfers between devices, body(): lax.all_to_all(jnp.stack([col_embed.astype(jnp.bfloat16)] * lax.axis_size...  12.5 us
    dot_general x2, matrix products, body(): lax.dot_general(block_rows, col_block, (((1,), (1,)), ((), ())), preferre...  11.7 us
    add x1, other arithmetic, body(): summed + jnp.where((owner_block == chosen[slot_id])[:, None], picked, jnp...  9.91 us
  transfers between devices with their start and end apart: 4, of which 2 were waited for; matrix products, arithmetic and copies ran while one was open for 26% of the time, Pallas kernels for 0%

profile of v1, /device:TPU:2, one launch (start us, length us, event | category | flops | bytes accessed | tf_op | source)
XLA Modules:
  0.0 364.7 jit_solution(5300683138511772872)
XLA Ops:
  7.2 0.9 convert_bitcast_fusion
  8.1 2.5 stack.2
  10.6 12.5 %all-to-all-start = ((bf16[64,1,64,512]{3,2,1,0:T(8,128)(2,1)}), bf16[64,1,64,512]{3,2,1,0:T(8,128)(2,1)}, u32[]{:S(2)}, u32[]{:S(2)}) async-start(bf16[64,1,64,512]{3,2,1,0:T(8,128)(2,1)} %stack.2), calls=%async_computation | async-start | bytes 8388608 | tf_op jit(solution)/shard_map/all_to_all | solution.py:41
  23.1 0.7 convert_element_type.40
  24.0 0.6 fusion.19
  25.9 8.3 %fusion.18 = (s32[1,1,1,1024,1024]{4,3,2,1,0:T(8,128)}, s32[1,1,1,1024,1024]{4,3,2,1,0:T(8,128)}) fusion(s32[1,1,2,1024,1024]{4,3,2,1,0:T(8,128)} %param.19), kind=kLoop, calls=%fused_computation.56 | loop fusion | bytes 16777216 | tf_op jit(solution)/shard_map/slice | solution.py:66
  34.2 5.4 %copy.22 = s32[1,1,1,1024,1024]{3,4,2,1,0:T(8,128)} copy(s32[1,1,1,1024,1024]{4,3,2,1,0:T(8,128)} %get-tuple-element.10) | data formatting | bytes 8388608
  40.2 5.4 %copy.23 = s32[1,1,1,1024,1024]{3,4,2,1,0:T(8,128)} copy(s32[1,1,1,1024,1024]{4,3,2,1,0:T(8,128)} %get-tuple-element.9) | data formatting | bytes 8388608
  45.7 1.4 compare_select_fusion
  47.0 72.3 %all-to-all-done = bf16[64,1,64,512]{3,2,1,0:T(8,128)(2,1)} async-done(((bf16[64,1,64,512]{3,2,1,0:T(8,128)(2,1)}), bf16[64,1,64,512]{3,2,1,0:T(8,128)(2,1)}, u32[]{:S(2)}, u32[]{:S(2)}) %all-to-all-start) | async-done | bytes 4194336 | tf_op jit(solution)/shard_map/all_to_all | solution.py:41
  119.3 19.4 %scatter_custom_fusion = bf16[2048,512]{1,0:T(8,128)(2,1)S(1)} fusion(s32[4096]{0:T(1024)S(1)} %bitcast.43, bf16[4096,512]{1,0:T(8,128)(2,1)} %bitcast.6, bf16[]{:T(256)} %constant.64.clone.1), kind=kCustom, calls=%fused_computation.13 | custom fusion | bytes 2097664 | tf_op jit(solution)/shard_map/scatter | solution.py:55
  138.8 7.6 %multiply_convert_fusion.1 = bf16[1024,1024]{0,1:T(8,128)(2,1)S(1)} fusion(s32[1,1,1,1024,1024]{3,4,2,1,0:T(8,128)} %copy.22, bf16[1024,512]{1,0:T(8,128)(2,1)} %all-gather.2.cloned.1.call-done, f32[1024]{0:T(1024)S(1)} %bitcast.45, f32[1024]{0:T(1024)S(1)} %log_subtract_fusion, bf16[2048,512]{1,0:T(8,128)(2,1)S(1)} %scatter_custom_fusion), kind=kOutput, calls=%fused_computation.11 | convolution fusion | flops 1089470464 | bytes 8396800 | tf_op jit(solution)/shard_map/dot_general | solution.py:63
  146.4 1.3 fusion.5
  147.7 0.1 copy-done.11
  147.7 1.6 copy-done
  149.3 0.3 copy-done.9
  149.6 4.1 %multiply_convert_fusion = bf16[1024,1024]{0,1:T(8,128)(2,1)S(1)} fusion(s32[1,1,1,1024,1024]{3,4,2,1,0:T(8,128)S(1)} %copy-done, bf16[1024,512]{1,0:T(8,128)(2,1)S(1)} %copy-done.9, f32[1024]{0:T(1024)S(1)} %bitcast.44, f32[1024]{0:T(1024)S(1)} %log_subtract_fusion, bf16[2048,512]{1,0:T(8,128)(2,1)S(1)} %scatter_custom_fusion), kind=kOutput, calls=%fused_computation.10 | convolution fusion | flops 1089470464 | bytes 8396800 | tf_op jit(solution)/shard_map/dot_general | solution.py:63
  153.8 1.3 copy-done.10
  155.1 2.6 convolution_add_fusion
  157.8 1.3 fusion.11
  159.1 3.1 fusion.21
  162.2 16.8 %gather_fusion.1 = f32[4096,512]{1,0:T(8,128)} fusion(f32[1024,512]{1,0:T(8,128)S(1)} %fusion.21, s32[4096]{0:T(1024)S(1)} %fusion.16), kind=kCustom, calls=%fused_computation.1.clone | custom fusion | bytes 16793600 | tf_op jit(solution)/shard_map/jit(_take)/gather | solution.py:78
  179.0 3.1 fusion.20
  182.1 16.8 %gather_fusion = f32[4096,512]{1,0:T(8,128)} fusion(f32[1024,512]{1,0:T(8,128)S(1)} %fusion.20, s32[4096]{0:T(1024)S(1)} %fusion.16), kind=kCustom, calls=%fused_computation.clone | custom fusion | bytes 16793600 | tf_op jit(solution)/shard_map/jit(_take)/gather | solution.py:78
  198.9 9.9 %fusion = f32[4096,512]{1,0:T(8,128)} fusion(f32[4096,512]{1,0:T(8,128)} %gather_fusion.1, f32[4096,512]{1,0:T(8,128)} %gather_fusion, pred[4096]{0:T(1024)(128)(4,1)S(1)} %compare_and_fusion, pred[4096]{0:T(1024)(128)(4,1)S(1)} %get-tuple-element.15, pred[4096]{0:T(1024)(128)(4,1)S(1)} %get-tuple-element.16), kind=kLoop, calls=%fused_computation.4 | loop fusion | flops 10485760 | bytes 25178112 | tf_op jit(solution)/shard_map/add | solution.py:79
  208.9 0.6 copy-done.7
  209.5 0.2 compare_reduce_fusion
  209.7 0.1 fusion.17
  209.8 0.1 copy-done.2
  209.9 2.2 multiply_subtract_fusion
  212.1 144.5 %reduce-scatter.5.cloned.1.call-done = f32[64,512]{1,0:T(8,128)} async-done(((f32[4096,512]{1,0:T(8,128)}), f32[64,512]{1,0:T(8,128)}) %reduce-scatter.5.cloned.1.call-update) | async-done | bytes 131088 | tf_op jit(solution)/shard_map/reduce_scatter | solution.py:82
  356.6 1.6 fusion.8
  (32 shorter events, 0.3 us)
Async XLA Ops:
  10.6 12.6 %copy-start.1 = (f32[256,512]{1,0:T(8,128)S(1)}, f32[256,512]{1,0:T(8,128)}, u32[]{:S(2)}) copy-start(f32[256,512]{1,0:T(8,128)} %param.12) | copy-start | bytes 1572868
  10.6 13.4 %copy-start.8 = (s32[1,1,2]{2,1,0:T(1,128)S(1)}, s32[1,1,2]{2,1,0:T(1,128)}, u32[]{:S(2)}) copy-start(s32[1,1,2]{2,1,0:T(1,128)} %param.18) | copy-start | bytes 28
  10.6 108.7 %all-to-all-start = ((bf16[64,1,64,512]{3,2,1,0:T(8,128)(2,1)}), bf16[64,1,64,512]{3,2,1,0:T(8,128)(2,1)}, u32[]{:S(2)}, u32[]{:S(2)}) async-start(bf16[64,1,64,512]{3,2,1,0:T(8,128)(2,1)} %stack.2), calls=%async_computation | async-start | bytes 8388608 | tf_op jit(solution)/shard_map/all_to_all | solution.py:41
  23.1 115.7 %all-gather.2.cloned.1.call-start = ((), (), s32[]{:S(2)}) async-start(), calls=%async_computation.3 | async-start | bytes 1310720 | tf_op jit(solution)/shard_map/all_gather | solution.py:39
  23.9 185.9 %reduce-scatter.3.cloned.1.call-start = ((), (), s32[]{:S(2)}) async-start(), calls=%async_computation.4 | async-start | bytes 2621440 | tf_op jit(solution)/shard_map/reduce_scatter | solution.py:83
  40.2 5.4 %copy-start.5 = (s32[1,4096]{1,0:T(1,128)S(1)}, s32[1,4096]{1,0:T(1,128)}, u32[]{:S(2)}) copy-start(s32[1,4096]{1,0:T(1,128)} %param.16) | copy-start | bytes 49156
  40.2 5.5 %copy-start.6 = (s32[1024]{0:T(1024)S(1)}, s32[1024]{0:T(1024)}, u32[]{:S(2)}) copy-start(s32[1024]{0:T(1024)} %param.17) | copy-start | bytes 12292
  146.4 1.4 copy-start.11
  146.4 2.9 copy-start
  146.4 3.2 copy-start.9
  153.7 1.3 copy-start.10
  157.7 198.9 %reduce-scatter.5.cloned.1.call-start = ((), (), s32[]{:S(2)}) async-start(), calls=%async_computation.5 | async-start | bytes 8519680 | tf_op jit(solution)/shard_map/reduce_scatter | solution.py:82
  208.8 0.7 copy-start.7
  208.8 1.1 copy-start.2
  208.8 147.8 %copy-start.3 = (f32[1,64,512]{2,1,0:T(8,128)S(1)}, f32[1,64,512]{2,1,0:T(8,128)}, u32[]{:S(2)}) copy-start(f32[1,64,512]{2,1,0:T(8,128)} %param.14) | copy-start | bytes 393220
  208.8 147.7 %copy-start.4 = (f32[1,64,512]{2,1,0:T(8,128)S(1)}, f32[1,64,512]{2,1,0:T(8,128)}, u32[]{:S(2)}) copy-start(f32[1,64,512]{2,1,0:T(8,128)} %param.15) | copy-start | bytes 393220
Sparse Core Ops, SparseCore 0:
  26.3 26.3 all-gather.1
  157.8 27.0 reduce-scatter.2
  209.0 147.5 reduce-scatter.4
